TPU v7x, 32 devices: a whole 2x2x4 slice. The times are simulated.
32 devices in a mesh: dp: 8 (over z, x), expert: 4 (over y, core).
Axes of the slice: x: 2, y: 2, z: 4, core: 2. Of those that a mesh axis runs over, the one named last changes fastest.
Arguments:
- tokens_in: bfloat16 [2, 8192, 768], P(None, ('dp', 'expert')), may hold values from -6 to 6
- out_grad: bfloat16 [2, 8192, 768], P(None, ('dp', 'expert')), may hold values from -6 to 6
- segments: int32 [2, 8192], P(None, ('dp', 'expert')), may hold values from 0 to 2, as said below
- expert_ids: int32 [2, 8192, 1], P(None, ('dp', 'expert')), may hold values from 0 to 7; in each aligned block of 256 rows (0 to 255, 256 to 511, ..., all dimensions but the last counted through in order) at most 64 rows name the same one
- gate_values: float32 [2, 8192], P(None, ('dp', 'expert')), may hold values from 0.5 to 1
- norm_gains: float32 [2, 768], replicated, may hold values from 0.5 to 1.5
- rel_bias: float32 [32, 12], replicated, may hold values from -3 to 3
- qkv_weight: float32 [768, 2304], P(('dp', 'expert')), may hold values from -0.21875 to 0.21875
- proj_weight: float32 [768, 768], P(('dp', 'expert')), may hold values from -3.5 to 3.5
- expert_in: float32 [8, 768, 3072], P('expert', 'dp'), may hold values from -0.21875 to 0.21875
- expert_out: float32 [8, 3072, 768], P('expert', 'dp'), may hold values from -0.15625 to 0.15625
- first_gains: float32 [2, 768], replicated
- second_gains: float32 [2, 768], replicated, as said below
- first_bias: float32 [32, 12], replicated
- second_bias: float32 [32, 12], replicated, as said below
- first_qkv: float32 [768, 2304], P(('dp', 'expert'))
- second_qkv: float32 [768, 2304], P(('dp', 'expert')), as said below
- first_proj: float32 [768, 768], P(('dp', 'expert'))
- second_proj: float32 [768, 768], P(('dp', 'expert')), as said below
- first_in: float32 [8, 768, 3072], P('expert', 'dp')
- second_in: float32 [8, 768, 3072], P('expert', 'dp'), as said below
- first_out: float32 [8, 3072, 768], P('expert', 'dp')
- second_out: float32 [8, 3072, 768], P('expert', 'dp'), as said below
Outputs:
- block_out: float32 [2, 8192, 768], P(None, ('dp', 'expert'))
- input_grad: float32 [2, 8192, 768], P(None, ('dp', 'expert'))
- grad_gains: float32 [2, 768], replicated
- grad_bias: float32 [32, 12], replicated
- grad_qkv: float32 [768, 2304], P(('dp', 'expert'))
- grad_proj: float32 [768, 768], P(('dp', 'expert'))
- grad_in: float32 [8, 768, 3072], P('expert', 'dp')
- grad_out: float32 [8, 3072, 768], P('expert', 'dp')
- new_gains: float32 [2, 768], replicated
- updated_relative_bias: float32 [32, 12], replicated
- new_qkv: float32 [768, 2304], P(('dp', 'expert'))
- new_proj: float32 [768, 768], P(('dp', 'expert'))
- new_in: float32 [8, 768, 3072], P('expert', 'dp')
- new_out: float32 [8, 3072, 768], P('expert', 'dp')
- moment_gains: float32 [2, 768], replicated
- moment_bias: float32 [32, 12], replicated
- moment_qkv: float32 [768, 2304], P(('dp', 'expert'))
- moment_proj: float32 [768, 768], P(('dp', 'expert'))
- moment_in: float32 [8, 768, 3072], P('expert', 'dp')
- moment_out: float32 [8, 3072, 768], P('expert', 'dp')
Inputs may be any that keep to these rules, and one draw needn't show every extreme that they name: `segments`: along each sequence of 1024 tokens the numbers never fall; number 1 begins within the sequence's first 256 tokens and ends within its last 256, so that numbers 0 and 2 are both present. `expert_ids`: in each aligned block of 256 tokens of a micro-batch (one device's tokens) at most 64 tokens name one expert. `second_gains`: Positive. `second_bias`: Positive. `second_qkv`: Positive. `second_proj`: Positive. `second_in`: Positive. `second_out`: Positive.
All inputs are finite; a program needn't handle non-finite values.
Results may differ from a plain program's by a relative error of at most 0.015.
Values may be sent and summed in bfloat16 or wider, within the bound.
A program may use at most 320 MiB of HBM per device.

v0:
```python
import jax
import jax.numpy as jnp
from jax import lax
from jax.sharding import PartitionSpec as P

BUCKETS = 32
STEP = 10


EPS_NORM = 1e-06
MASKED = -1000000000.0
LIMITS = (12, 16, 23, 32, 46, 64, 91)
UPPER_PRECISION = lax.Precision.HIGHEST


def rms_norm(inputs, gain_vec):
    inv_rms = lax.rsqrt(jnp.mean(inputs * inputs, axis=-1, keepdims=True) + EPS_NORM)
    return inputs * inv_rms * gain_vec


def exact_gelu(inputs):
    return jax.nn.gelu(inputs, approximate=False)


def bucket_of(query_position_index, key_position_index):
    offset = key_position_index[None, :] - query_position_index[:, None]
    distance = jnp.abs(offset)
    far_bucket = 8 + sum(((distance >= bound_at).astype(jnp.int32) for bound_at in LIMITS))
    return jnp.where(distance < 8, distance, far_bucket) + jnp.where(offset > 0, 16, 0)


def bucket_onehot_matrix(query_position_index, key_position_index):
    buckets = bucket_of(query_position_index, key_position_index)
    return (buckets[None] == jnp.arange(BUCKETS, dtype=jnp.int32)[:, None, None]).astype(
        jnp.float32
    )


def position_bias(bias_lookup_table, query_position_index, seq_len):
    block_width = min(512, seq_len)
    block_count = seq_len // block_width
    head_count = bias_lookup_table.shape[1]

    def position_one_block(key_start):
        key_position_index = key_start + jnp.arange(block_width, dtype=jnp.int32)
        return jnp.einsum(
            "vg,vjs->gjs",
            bias_lookup_table,
            bucket_onehot_matrix(query_position_index, key_position_index),
            precision=UPPER_PRECISION,
        )

    pieces = lax.map(position_one_block, jnp.arange(block_count, dtype=jnp.int32) * block_width)
    return jnp.transpose(pieces, (1, 2, 0, 3)).reshape(
        head_count, query_position_index.shape[0], seq_len
    )


def table_grad(grad_logits, query_position_index, seq_len):
    block_width = min(512, seq_len)
    block_count = seq_len // block_width
    head_count, query_rows = (grad_logits.shape[0], grad_logits.shape[1])
    pieces = jnp.transpose(
        grad_logits.reshape(head_count, query_rows, block_count, block_width), (2, 0, 1, 3)
    )

    def table_one_block(running, operands):
        key_start, current_piece = operands
        key_position_index = key_start + jnp.arange(block_width, dtype=jnp.int32)
        return (
            running
            + jnp.einsum(
                "uei,sei->su",
                current_piece,
                bucket_onehot_matrix(query_position_index, key_position_index),
                precision=UPPER_PRECISION,
            ),
            None,
        )

    starts = jnp.arange(block_count, dtype=jnp.int32) * block_width
    running, unused = lax.scan(
        table_one_block, jnp.zeros((BUCKETS, head_count), jnp.float32), (starts, pieces)
    )
    return running


def attention_scores(q_heads, k_heads, pos_bias, allowed, score_scale):
    raw_scores = jnp.einsum("qhd,khd->hqk", q_heads, k_heads, preferred_element_type=jnp.float32)
    return jnp.where(allowed[None], score_scale * raw_scores + pos_bias, MASKED)


def slot_index(chosen, expert_count, capacity):
    hot_rows = (chosen[:, None] == jnp.arange(expert_count, dtype=jnp.int32)[None, :]).astype(
        jnp.int32
    )
    rank_in = jnp.sum((jnp.cumsum(hot_rows, axis=0) - 1) * hot_rows, axis=1)
    return chosen * capacity + rank_in


def adam_step(weight, gradient, first_mom, second, step_rate):
    first_new = 0.9 * first_mom + 0.1 * gradient
    second_new = 0.999 * second + 0.001 * gradient * gradient
    first_hat = first_new / (1.0 - 0.9**STEP)
    second_hat = second_new / (1.0 - 0.999**STEP)
    updated = weight - step_rate * (first_hat / (jnp.sqrt(second_hat) + 1e-08) + 0.01 * weight)
    return (updated, second_new)


def local(
    tokens_in,
    out_grad,
    segments,
    expert_ids,
    gate_values,
    norm_gains,
    rel_bias,
    qkv_weight,
    proj_weight,
    expert_in,
    expert_out,
    first_gains,
    second_gains,
    first_bias,
    second_bias,
    first_qkv,
    second_qkv,
    first_proj,
    second_proj,
    first_in,
    second_in,
    first_out,
    second_out,
):
    groups = lax.axis_size("expert")
    micros, tok_rows, model_width = tokens_in.shape
    seq_len = tok_rows * groups
    head_count = rel_bias.shape[1]
    head_dim = model_width // head_count
    local_experts = expert_in.shape[0]
    hidden_units = expert_in.shape[2]
    expert_count = local_experts * groups
    capacity = 2 * tok_rows // expert_count
    score_scale = head_dim ** (-0.5)
    query_position_index = lax.axis_index("expert") * tok_rows + jnp.arange(
        tok_rows, dtype=jnp.int32
    )
    pos_bias = position_bias(rel_bias, query_position_index, seq_len)
    qkv_low = qkv_weight.astype(jnp.bfloat16)
    proj_low = proj_weight.astype(jnp.bfloat16)
    in_low = expert_in.astype(jnp.bfloat16)
    out_low = expert_out.astype(jnp.bfloat16)
    acc_qkv = jnp.zeros((model_width, 3 * model_width), jnp.float32)
    acc_proj = jnp.zeros((model_width, model_width), jnp.float32)
    acc_in = jnp.zeros((local_experts, model_width, hidden_units), jnp.float32)
    acc_out = jnp.zeros((local_experts, hidden_units, model_width), jnp.float32)
    acc_gains = jnp.zeros((2, model_width), jnp.float32)
    acc_table = jnp.zeros(rel_bias.shape, jnp.float32)
    block_outs = []
    input_grads = []
    for micro_idx in range(micros):
        dense_qkv, dense_proj = (
            lax.all_gather(qkv_low, ("dp", "expert"), axis=0, tiled=True),
            lax.all_gather(proj_low, ("dp", "expert"), axis=0, tiled=True),
        )
        exp_in, exp_out = (
            lax.all_gather(in_low, "dp", axis=1, tiled=True),
            lax.all_gather(out_low, "dp", axis=1, tiled=True),
        )
        residual = tokens_in[micro_idx].astype(jnp.float32)
        normed, norm_back_one = jax.vjp(rms_norm, residual, norm_gains[0])
        act_one = normed.astype(jnp.bfloat16)
        qkv_all = jnp.dot(act_one, dense_qkv, preferred_element_type=jnp.float32).astype(
            jnp.bfloat16
        )
        queries = qkv_all[:, :model_width]
        keys_local = qkv_all[:, model_width : 2 * model_width]
        values_local = qkv_all[:, 2 * model_width :]
        seg_local = segments[micro_idx]
        keys_all, values_all, seg_all = (
            lax.all_gather(keys_local, "expert", axis=0, tiled=True),
            lax.all_gather(values_local, "expert", axis=0, tiled=True),
            lax.all_gather(seg_local.astype(jnp.bfloat16), "expert", axis=0, tiled=True),
        )
        allowed = seg_local[:, None] == seg_all.astype(jnp.int32)[None, :]
        q_heads = queries.reshape(tok_rows, head_count, head_dim)
        k_heads = keys_all.reshape(seq_len, head_count, head_dim)
        v_heads = values_all.reshape(seq_len, head_count, head_dim)
        logits = attention_scores(q_heads, k_heads, pos_bias, allowed, score_scale)
        row_max = jnp.max(logits, axis=-1, keepdims=True)
        log_total = row_max + jnp.log(jnp.sum(jnp.exp(logits - row_max), axis=-1, keepdims=True))
        probs_low = jnp.exp(logits - log_total).astype(jnp.bfloat16)
        mixed_out = (
            jnp.einsum("hqk,khd->qhd", probs_low, v_heads, preferred_element_type=jnp.float32)
            .astype(jnp.bfloat16)
            .reshape(tok_rows, model_width)
        )
        hidden = residual + jnp.dot(mixed_out, dense_proj, preferred_element_type=jnp.float32)
        normed_two, norm_back_two = jax.vjp(rms_norm, hidden, norm_gains[1])
        routed = normed_two.astype(jnp.bfloat16)
        slot_rows = slot_index(expert_ids[micro_idx][:, 0], expert_count, capacity)
        send_buf = (
            jnp.zeros((expert_count * capacity, model_width), jnp.bfloat16)
            .at[slot_rows]
            .set(routed)
        )
        send_buf = send_buf.reshape(groups, local_experts, capacity, model_width)
        arrived_rows = lax.all_to_all(send_buf, "expert", split_axis=0, concat_axis=0, tiled=True)
        pre_act = jnp.einsum(
            "secd,edf->secf", arrived_rows, exp_in, preferred_element_type=jnp.float32
        )
        post_act = exact_gelu(pre_act).astype(jnp.bfloat16)
        result = jnp.einsum(
            "secf,efd->secd", post_act, exp_out, preferred_element_type=jnp.float32
        ).astype(jnp.bfloat16)
        returned = lax.all_to_all(
            result, "expert", split_axis=0, concat_axis=0, tiled=True
        ).reshape(expert_count * capacity, model_width)
        gate_col = gate_values[micro_idx][:, None]
        block_outs.append(hidden + gate_col * returned[slot_rows].astype(jnp.float32))
        dense_qkv, dense_proj = (
            lax.all_gather(qkv_low, ("dp", "expert"), axis=0, tiled=True),
            lax.all_gather(proj_low, ("dp", "expert"), axis=0, tiled=True),
        )
        exp_in, exp_out = (
            lax.all_gather(in_low, "dp", axis=1, tiled=True),
            lax.all_gather(out_low, "dp", axis=1, tiled=True),
        )
        grad_top = out_grad[micro_idx].astype(jnp.float32)
        back_send = (
            jnp.zeros((expert_count * capacity, model_width), jnp.bfloat16)
            .at[slot_rows]
            .set((gate_col * grad_top).astype(jnp.bfloat16))
        )
        back_send = back_send.reshape(groups, local_experts, capacity, model_width)
        grad_res = lax.all_to_all(back_send, "expert", split_axis=0, concat_axis=0, tiled=True)
        post_act, gelu_back = jax.vjp(exact_gelu, pre_act)
        acc_out = acc_out + jnp.einsum(
            "secf,secd->efd",
            post_act.astype(jnp.bfloat16),
            grad_res,
            preferred_element_type=jnp.float32,
        )
        grad_post = jnp.einsum(
            "secd,efd->secf", grad_res, exp_out, preferred_element_type=jnp.float32
        )
        grad_pre = gelu_back(grad_post)[0].astype(jnp.bfloat16)
        acc_in = acc_in + jnp.einsum(
            "secd,secf->edf", arrived_rows, grad_pre, preferred_element_type=jnp.float32
        )
        grad_piece = jnp.einsum(
            "secf,edf->secd", grad_pre, exp_in, preferred_element_type=jnp.float32
        ).astype(jnp.bfloat16)
        grad_back = lax.all_to_all(
            grad_piece, "expert", split_axis=0, concat_axis=0, tiled=True
        ).reshape(expert_count * capacity, model_width)
        grad_hidden_n, grad_gain_two = norm_back_two(grad_back[slot_rows].astype(jnp.float32))
        grad_hidden = grad_top + grad_hidden_n
        grad_attn = grad_hidden.astype(jnp.bfloat16)
        acc_proj = acc_proj + jnp.dot(mixed_out.T, grad_attn, preferred_element_type=jnp.float32)
        grad_mixed = (
            jnp.dot(grad_attn, dense_proj.T, preferred_element_type=jnp.float32)
            .astype(jnp.bfloat16)
            .reshape(tok_rows, head_count, head_dim)
        )
        logits = attention_scores(q_heads, k_heads, pos_bias, allowed, score_scale)
        attn_probs = jnp.exp(logits - log_total)
        grad_vals = jnp.einsum(
            "hqk,qhd->khd",
            attn_probs.astype(jnp.bfloat16),
            grad_mixed,
            preferred_element_type=jnp.float32,
        )
        grad_probs = jnp.einsum(
            "qhd,khd->hqk", grad_mixed, v_heads, preferred_element_type=jnp.float32
        )
        grad_logits = attn_probs * (
            grad_probs - jnp.sum(attn_probs * grad_probs, axis=-1, keepdims=True)
        )
        acc_table = acc_table + table_grad(grad_logits, query_position_index, seq_len)
        grad_raw = (score_scale * grad_logits).astype(jnp.bfloat16)
        grad_query = (
            jnp.einsum("hqk,khd->qhd", grad_raw, k_heads, preferred_element_type=jnp.float32)
            .astype(jnp.bfloat16)
            .reshape(tok_rows, model_width)
        )
        grad_keys = jnp.einsum(
            "hqk,qhd->khd", grad_raw, q_heads, preferred_element_type=jnp.float32
        ).reshape(seq_len, model_width)
        key_grad, value_grad = (
            lax.psum_scatter(
                grad_keys.astype(jnp.bfloat16), "expert", scatter_dimension=0, tiled=True
            ).astype(jnp.float32),
            lax.psum_scatter(
                grad_vals.reshape(seq_len, model_width).astype(jnp.bfloat16),
                "expert",
                scatter_dimension=0,
                tiled=True,
            ).astype(jnp.float32),
        )
        grad_qkv_rows = jnp.concatenate(
            [grad_query, key_grad.astype(jnp.bfloat16), value_grad.astype(jnp.bfloat16)], axis=1
        )
        acc_qkv = acc_qkv + jnp.dot(act_one.T, grad_qkv_rows, preferred_element_type=jnp.float32)
        grad_normed = jnp.dot(grad_qkv_rows, dense_qkv.T, preferred_element_type=jnp.float32)
        grad_resid_n, grad_gain_one = norm_back_one(grad_normed)
        input_grads.append(grad_hidden + grad_resid_n)
        acc_gains = acc_gains + jnp.stack([grad_gain_one, grad_gain_two])
    grad_qkv, grad_proj = (
        lax.psum_scatter(acc_qkv, ("dp", "expert"), scatter_dimension=0, tiled=True),
        lax.psum_scatter(acc_proj, ("dp", "expert"), scatter_dimension=0, tiled=True),
    )
    grad_in, grad_out = (
        lax.psum_scatter(acc_in.astype(jnp.bfloat16), "dp", scatter_dimension=1, tiled=True).astype(
            jnp.float32
        ),
        lax.psum_scatter(
            acc_out.astype(jnp.bfloat16), "dp", scatter_dimension=1, tiled=True
        ).astype(jnp.float32),
    )
    grad_gains, grad_bias = lax.psum((acc_gains, acc_table), ("dp", "expert"))
    fan_proj = max(1, 4 * model_width // seq_len)
    new_gains, moment_gains = adam_step(norm_gains, grad_gains, first_gains, second_gains, 0.25)
    updated_relative_bias, moment_bias = adam_step(
        rel_bias, grad_bias, first_bias, second_bias, 0.5
    )
    new_qkv, moment_qkv = adam_step(
        qkv_weight, grad_qkv, first_qkv, second_qkv, model_width ** (-0.5)
    )
    new_proj, moment_proj = adam_step(
        proj_weight, grad_proj, first_proj, second_proj, fan_proj ** (-0.5)
    )
    new_in, moment_in = adam_step(expert_in, grad_in, first_in, second_in, model_width ** (-0.5))
    new_out, moment_out = adam_step(
        expert_out, grad_out, first_out, second_out, (hidden_units // 2) ** (-0.5)
    )
    return (
        jnp.stack(block_outs),
        jnp.stack(input_grads),
        grad_gains,
        grad_bias,
        grad_qkv,
        grad_proj,
        grad_in,
        grad_out,
        new_gains,
        updated_relative_bias,
        new_qkv,
        new_proj,
        new_in,
        new_out,
        moment_gains,
        moment_bias,
        moment_qkv,
        moment_proj,
        moment_in,
        moment_out,
    )


def solution(mesh):
    placed = (
        P(None, ("dp", "expert"), None),
        P(None, ("dp", "expert"), None),
        P(None, ("dp", "expert")),
        P(None, ("dp", "expert"), None),
        P(None, ("dp", "expert")),
        P(),
        P(),
        P(("dp", "expert"), None),
        P(("dp", "expert"), None),
        P("expert", "dp", None),
        P("expert", "dp", None),
        P(),
        P(),
        P(),
        P(),
        P(("dp", "expert"), None),
        P(("dp", "expert"), None),
        P(("dp", "expert"), None),
        P(("dp", "expert"), None),
        P("expert", "dp", None),
        P("expert", "dp", None),
        P("expert", "dp", None),
        P("expert", "dp", None),
    )
    return jax.shard_map(
        local,
        mesh=mesh,
        in_specs=placed,
        out_specs=(
            P(None, ("dp", "expert"), None),
            P(None, ("dp", "expert"), None),
            P(),
            P(),
            P(("dp", "expert"), None),
            P(("dp", "expert"), None),
            P("expert", "dp", None),
            P("expert", "dp", None),
            P(),
            P(),
            P(("dp", "expert"), None),
            P(("dp", "expert"), None),
            P("expert", "dp", None),
            P("expert", "dp", None),
            P(),
            P(),
            P(("dp", "expert"), None),
            P(("dp", "expert"), None),
            P("expert", "dp", None),
            P("expert", "dp", None),
        ),
        check_vma=False,
    )
```

profile of v0, /device:TPU:0, one launch (start us, length us, event | category | flops | bytes accessed | tf_op | source)
XLA Modules:
  0.0 1374.8 jit_solution(18226712983718219861)
XLA Ops:
  11.7 62.7 %all-gather.11.cloned.1.call-done = bf16[768,2304]{1,0:T(8,128)(2,1)} async-done(((bf16[24,2304]{1,0:T(8,128)(2,1)}), bf16[768,2304]{1,0:T(8,128)(2,1)}) %all-gather.11.cloned.1.call-update) | async-done | bytes 3538960 | tf_op jit(solution)/shard_map/all_gather | solution.py:163
  90.1 18.3 %while.33 = (s32[]{:T(128)}, f32[2,12,256,512]{3,1,2,0:T(8,128)}, s32[2]{0:T(128)S(1)}, f32[32,12]{0,1:T(8,128)S(1)}, s32[]{:T(128)}, /*index=5*/s32[]{:T(128)}) while((s32[]{:T(128)}, f32[2,12,256,512]{3,1,2,0:T(8,128)}, s32[2]{0:T(128)S(1)}, f32[32,12]{0,1:T(8,128)S(1)}, s32[]{:T(128)}, /*index=5*/s32[]{:T(128)}) %tuple.143), condition=%wide.region_2.3_spmd.clone, body=%wide.region_1.2_spmd.clone.sunk | while | flops 611844864 | bytes 9444965 | solution.py:53
  108.4 22.5 %copy.84 = f32[12,256,2,512]{3,2,1,0:T(2,128)} copy(f32[12,256,2,512]{3,0,1,2:T(8,128)} %bitcast.451) | data formatting | bytes 25165824 | tf_op jit(solution)/shard_map/transpose | solution.py:54
  131.0 17.1 %reshape.557 = f32[12,256,1024]{2,1,0:T(8,128)} reshape(f32[12,256,2,512]{3,2,1,0:T(2,128)} %copy.84) | data formatting | bytes 25165824 | tf_op jit(solution)/shard_map/reshape | solution.py:54
  198.9 19.9 %all-gather.25.cloned.1.call-done = bf16[1024,768]{1,0:T(8,128)(2,1)} async-done(((bf16[256,768]{1,0:T(8,128)(2,1)}), bf16[1024,768]{1,0:T(8,128)(2,1)}) %all-gather.25.cloned.1.call-update) | async-done | bytes 1572880 | tf_op jit(solution)/shard_map/all_gather | solution.py:181
  242.2 117.6 %all-gather.19.cloned.1.call-done = bf16[2,768,3072]{2,1,0:T(8,128)(2,1)} async-done(((bf16[2,96,3072]{2,1,0:T(8,128)(2,1)}), bf16[2,768,3072]{2,1,0:T(8,128)(2,1)}) %all-gather.19.cloned.1.call-update) | async-done | bytes 9437200 | tf_op jit(solution)/shard_map/all_gather | solution.py:167
  359.7 19.0 %fusion.102 = (bf16[4,2,64,3072]{3,2,0,1:T(8,128)(2,1)}, f32[4,2,64,3072]{3,2,0,1:T(8,128)}, f32[2,4,64,3072]{3,2,1,0:T(8,128)}) fusion(bf16[2,768,3072]{2,1,0:T(8,128)(2,1)} %all-gather.19.cloned.1.call-done, bf16[4,2,64,768]{3,2,1,0:T(8,128)(2,1)} %all-to-all-done), kind=kOutput, calls=%fused_computation.146 | convolution fusion | flops 2518155264 | bytes 25952256 | tf_op jit(solution)/shard_map/secd,edf->secf/dot_general | solution.py:209
  382.4 18.9 %fusion.100 = (bf16[4,2,64,3072]{3,2,0,1:T(8,128)(2,1)}, f32[4,2,64,3072]{3,2,0,1:T(8,128)}, f32[2,4,64,3072]{3,2,1,0:T(8,128)}) fusion(bf16[2,768,3072]{2,1,0:T(8,128)(2,1)} %all-gather.19.cloned.1.call-done, bf16[4,2,64,768]{3,2,1,0:T(8,128)(2,1)S(1)} %all-to-all-done.2), kind=kOutput, calls=%fused_computation.139 | convolution fusion | flops 2518155264 | bytes 25952256 | tf_op jit(solution)/shard_map/secd,edf->secf/dot_general | solution.py:209
  404.9 11.0 fusion.216
  417.3 13.6 fusion.57
  431.3 161.4 %reduce-scatter.23.cloned.1.call-done = bf16[2,384,768]{2,1,0:T(8,128)(2,1)} async-done(((bf16[2,3072,768]{2,1,0:T(8,128)(2,1)}), bf16[2,384,768]{2,1,0:T(8,128)(2,1)}) %reduce-scatter.23.cloned.1.call-update) | async-done | bytes 1179664 | tf_op jit(solution)/shard_map/reduce_scatter | solution.py:317
  599.9 136.7 %all-gather.21.cloned.1.call-done = bf16[2,3072,768]{2,1,0:T(8,128)(2,1)} async-done(((bf16[2,384,768]{2,1,0:T(8,128)(2,1)}), bf16[2,3072,768]{2,1,0:T(8,128)(2,1)}) %all-gather.21.cloned.1.call-update) | async-done | bytes 9437200 | tf_op jit(solution)/shard_map/all_gather | solution.py:168
  736.6 13.0 fusion.90
  761.7 13.5 fusion.97
  844.5 19.6 %subtract_multiply_fusion.1 = f32[12,256,1024]{2,1,0:T(8,128)} fusion(f32[12,256,1024]{2,1,0:T(8,128)} %copy-done, f32[12,256]{1,0:T(8,128)S(1)} %copy-done.53, bf16[256,12,64]{0,2,1:T(8,128)(2,1)S(1)} %bitcast.461, bf16[1024,12,64]{0,2,1:T(8,128)(2,1)S(1)} %bitcast.444), kind=kOutput, calls=%fused_computation.84 | convolution fusion | flops 821039104 | bytes 27144192 | tf_op jit(solution)/shard_map/sub | solution.py:278
  880.6 19.5 %subtract_multiply_fusion = f32[12,256,1024]{2,1,0:T(8,128)} fusion(f32[12,256,1024]{2,1,0:T(8,128)} %copy-done.1, f32[12,256]{1,0:T(8,128)S(1)} %copy-done.55, bf16[256,12,64]{0,2,1:T(8,128)(2,1)S(1)} %bitcast.463, bf16[1024,12,64]{0,2,1:T(8,128)(2,1)S(1)} %bitcast.446), kind=kOutput, calls=%fused_computation.80 | convolution fusion | flops 821039104 | bytes 27144192 | tf_op jit(solution)/shard_map/sub | solution.py:278
  932.1 31.5 %reduce-scatter.13.cloned.1.call-done = bf16[256,768]{0,1:T(8,128)(2,1)} async-done(((bf16[1024,768]{0,1:T(8,128)(2,1)}), bf16[256,768]{0,1:T(8,128)(2,1)}) %reduce-scatter.13.cloned.1.call-update) | async-done | bytes 393232 | tf_op jit(solution)/shard_map/reduce_scatter | solution.py:291
  971.1 11.4 fusion.134
  982.5 12.0 fusion.58
  994.5 16.9 %reshape.581 = f32[12,256,2,512]{3,2,1,0:T(2,128)} reshape(f32[12,256,1024]{2,1,0:T(8,128)} %subtract_multiply_fusion.1) | data formatting | bytes 25165824 | tf_op jit(solution)/shard_map/reshape | solution.py:64
  1011.4 17.1 %reshape.582 = f32[12,256,2,512]{3,2,1,0:T(2,128)} reshape(f32[12,256,1024]{2,1,0:T(8,128)} %subtract_multiply_fusion) | data formatting | bytes 25165824 | tf_op jit(solution)/shard_map/reshape | solution.py:64
  1029.7 18.0 %copy.135 = f32[12,256,2,512]{3,0,1,2:T(8,128)} copy(f32[12,256,2,512]{3,2,1,0:T(2,128)} %reshape.581) | data formatting | bytes 25165824 | tf_op jit(solution)/shard_map/reshape | solution.py:64
  1047.7 18.1 %copy.134 = f32[12,256,2,512]{3,0,1,2:T(8,128)} copy(f32[12,256,2,512]{3,2,1,0:T(2,128)} %reshape.582) | data formatting | bytes 25165824 | tf_op jit(solution)/shard_map/reshape | solution.py:64
  1065.8 26.1 %while.34 = (s32[]{:T(128)}, f32[32,12]{0,1:T(8,128)S(1)}, s32[2]{0:T(128)S(1)}, f32[2,12,256,512]{3,1,2,0:T(8,128)}, s32[]{:T(128)}, /*index=5*/s32[]{:T(128)}, s32[]{:T(128)}) while((s32[]{:T(128)}, f32[32,12]{0,1:T(8,128)S(1)}, s32[2]{0:T(128)S(1)}, f32[2,12,256,512]{3,1,2,0:T(8,128)}, s32[]{:T(128)}, /*index=5*/s32[]{:T(128)}, ...), condition=%wide.region_36.37_spmd.clone, body=%wide.region_35.36_spmd.clone.sunk | while | flops 611845632 | bytes 9446519 | solution.py:82
  1067.6 11.1 fusion.338
  1080.6 11.3 fusion.338
  1091.9 26.4 %while.35 = (s32[]{:T(128)}, f32[32,12]{0,1:T(8,128)S(1)}, s32[2]{0:T(128)S(1)}, f32[2,12,256,512]{3,1,2,0:T(8,128)}, s32[]{:T(128)}, /*index=5*/s32[]{:T(128)}, s32[]{:T(128)}) while((s32[]{:T(128)}, f32[32,12]{0,1:T(8,128)S(1)}, s32[2]{0:T(128)S(1)}, f32[2,12,256,512]{3,1,2,0:T(8,128)}, s32[]{:T(128)}, /*index=5*/s32[]{:T(128)}, ...), condition=%wide.region_38.39_spmd.clone, body=%wide.region_37.38_spmd.clone.sunk | while | flops 611845632 | bytes 9446519 | solution.py:82
  1094.0 11.2 fusion.341
  1107.1 11.2 fusion.341
  1127.7 41.2 %all-reduce = (f32[2,768]{1,0:T(2,128)S(1)}, f32[32,12]{0,1:T(8,128)S(1)}) all-reduce(f32[2,768]{1,0:T(2,128)S(1)} %maximum_add_fusion, f32[32,12]{0,1:T(8,128)S(1)} %add.510), channel_id=1, replica_groups=mesh['dp'=8,'expert'=4] {'dp','expert'}, use_global_device_ids=true, to_apply=%region_34.35 | all-reduce | flops 1920 | bytes 15360 | tf_op jit(solution)/shard_map/psum | solution.py:321
  1175.6 19.5 %reduce-scatter.17.cloned.1.call-done = f32[24,2304]{1,0:T(8,128)} async-done(((f32[768,2304]{1,0:T(8,128)}), f32[24,2304]{1,0:T(8,128)}) %reduce-scatter.17.cloned.1.call-update) | async-done | bytes 221200 | tf_op jit(solution)/shard_map/reduce_scatter | solution.py:310
  1197.0 164.4 %reduce-scatter.21.cloned.1.call-done = bf16[2,96,3072]{2,1,0:T(8,128)(2,1)} async-done(((bf16[2,768,3072]{2,1,0:T(8,128)(2,1)}), bf16[2,96,3072]{2,1,0:T(8,128)(2,1)}) %reduce-scatter.21.cloned.1.call-update) | async-done | bytes 1179664 | tf_op jit(solution)/shard_map/reduce_scatter | solution.py:314
  (397 shorter events, 297.6 us)
Async XLA Ops:
  7.2 67.2 %all-gather.11.cloned.1.call-start = ((), (), s32[]{:S(2)}) async-start(), calls=%async_computation.16 | async-start | bytes 3649536 | tf_op jit(solution)/shard_map/all_gather | solution.py:163
  8.9 158.1 %all-gather.13.cloned.1.call-start = ((), (), s32[]{:S(2)}) async-start(), calls=%async_computation.17 | async-start | bytes 1966080 | tf_op jit(solution)/shard_map/all_gather | solution.py:182
  9.8 226.1 %copy-start.58 = (f32[768]{0:T(1024)}, f32[768]{0:T(1024)S(1)}, u32[]{:S(2)}) copy-start(f32[768]{0:T(1024)S(1)} %get-tuple-element.171) | copy-start | bytes 9220
  78.7 90.3 %all-gather.15.cloned.1.call-start = ((), (), s32[]{:S(2)}) async-start(), calls=%async_computation.18 | async-start | bytes 1966080 | tf_op jit(solution)/shard_map/all_gather | solution.py:181
  79.4 105.9 %all-gather.17.cloned.1.call-start = ((), (), s32[]{:S(2)}) async-start(), calls=%async_computation.19 | async-start | bytes 1216512 | tf_op jit(solution)/shard_map/all_gather | solution.py:164
  81.0 116.2 %all-gather.23.cloned.1.call-start = ((), (), s32[]{:S(2)}) async-start(), calls=%async_computation.22 | async-start | bytes 1966080 | tf_op jit(solution)/shard_map/all_gather | solution.py:182
  85.9 132.9 %all-gather.25.cloned.1.call-start = ((), (), s32[]{:S(2)}) async-start(), calls=%async_computation.23 | async-start | bytes 1966080 | tf_op jit(solution)/shard_map/all_gather | solution.py:181
  86.5 273.2 %all-gather.19.cloned.1.call-start = ((), (), s32[]{:S(2)}) async-start(), calls=%async_computation.20 | async-start | bytes 10616832 | tf_op jit(solution)/shard_map/all_gather | solution.py:167
  190.1 48.5 %all-to-all-start = ((bf16[4,2,64,768]{3,2,1,0:T(8,128)(2,1)}), bf16[4,2,64,768]{3,2,1,0:T(8,128)(2,1)}, u32[]{:S(2)}, u32[]{:S(2)}) async-start(bf16[4,2,64,768]{3,2,1,0:T(8,128)(2,1)} %bitcast.18), calls=%async_computation | async-start | bytes 1572864 | tf_op jit(solution)/shard_map/all_to_all | solution.py:208
  238.7 140.1 %all-to-all-start.2 = ((bf16[4,2,64,768]{3,2,1,0:T(8,128)(2,1)}), bf16[4,2,64,768]{3,2,1,0:T(8,128)(2,1)S(1)}, u32[]{:S(2)}, u32[]{:S(2)}) async-start(bf16[4,2,64,768]{3,2,1,0:T(8,128)(2,1)} %bitcast.45), calls=%async_computation.2 | async-start | bytes 1572864 | tf_op jit(solution)/shard_map/all_to_all | solution.py:208
  378.7 22.6 %all-to-all-start.4 = ((bf16[4,2,64,768]{3,2,1,0:T(8,128)(2,1)}), bf16[4,2,64,768]{3,2,1,0:T(8,128)(2,1)S(1)}, u32[]{:S(2)}, u32[]{:S(2)}) async-start(bf16[4,2,64,768]{3,2,1,0:T(8,128)(2,1)} %bitcast.55), calls=%async_computation.4 | async-start | bytes 1572864 | tf_op jit(solution)/shard_map/all_to_all | solution.py:236
  401.3 15.1 %all-to-all-start.6 = ((bf16[4,2,64,768]{3,2,1,0:T(8,128)(2,1)}), bf16[4,2,64,768]{3,2,1,0:T(8,128)(2,1)S(1)}, u32[]{:S(2)}, u32[]{:S(2)}) async-start(bf16[4,2,64,768]{3,2,1,0:T(8,128)(2,1)} %bitcast.69), calls=%async_computation.8 | async-start | bytes 1572864 | tf_op jit(solution)/shard_map/all_to_all | solution.py:236
  404.8 187.9 %reduce-scatter.23.cloned.1.call-start = ((), (), s32[]{:S(2)}) async-start(), calls=%async_computation.31 | async-start | bytes 10616832 | tf_op jit(solution)/shard_map/reduce_scatter | solution.py:317
  431.0 161.7 %copy-start.35 = (f32[2,384,768]{2,1,0:T(8,128)S(1)}, f32[2,384,768]{2,1,0:T(8,128)}, u32[]{:S(2)}) copy-start(f32[2,384,768]{2,1,0:T(8,128)} %param.39) | copy-start | bytes 7077892
  431.0 168.3 %copy-start.94 = (s32[256,1]{0,1:T(1,128)S(1)}, s32[256,1]{0,1:T(1,128)}, u32[]{:S(2)}) copy-start(s32[256,1]{0,1:T(1,128)} %copy-done.93) | copy-start | bytes 3076
  431.0 168.3 %copy-start.92 = (s32[256,1]{0,1:T(1,128)S(1)}, s32[256,1]{0,1:T(1,128)}, u32[]{:S(2)}) copy-start(s32[256,1]{0,1:T(1,128)} %copy-done.91) | copy-start | bytes 3076
  431.0 305.6 %all-gather.21.cloned.1.call-start = ((), (), s32[]{:S(2)}) async-start(), calls=%async_computation.21 | async-start | bytes 10616832 | tf_op jit(solution)/shard_map/all_gather | solution.py:168
  599.3 218.5 %copy-start.79 = (s32[1024]{0:T(1024)}, s32[1024]{0:T(1024)S(1)}, u32[]{:S(2)}) copy-start(s32[1024]{0:T(1024)S(1)} %pad_clamp_fusion.1) | copy-start | bytes 12292
  757.8 25.6 %all-to-all-start.7 = ((bf16[4,2,64,768]{3,2,1,0:T(8,128)(2,1)}), bf16[4,2,64,768]{3,2,1,0:T(8,128)(2,1)S(1)}, u32[]{:S(2)}, u32[]{:S(2)}) async-start(bf16[4,2,64,768]{3,2,1,0:T(8,128)(2,1)} %copy.96), calls=%async_computation.9 | async-start | bytes 1572864 | tf_op jit(solution)/shard_map/all_to_all | solution.py:254
  783.4 15.1 %all-to-all-start.3 = ((bf16[4,2,64,768]{3,2,1,0:T(8,128)(2,1)}), bf16[4,2,64,768]{3,2,1,0:T(8,128)(2,1)S(1)}, u32[]{:S(2)}, u32[]{:S(2)}) async-start(bf16[4,2,64,768]{3,2,1,0:T(8,128)(2,1)} %copy.91), calls=%async_computation.3 | async-start | bytes 1572864 | tf_op jit(solution)/shard_map/all_to_all | solution.py:216
  798.5 15.4 %all-to-all-start.5 = ((bf16[4,2,64,768]{3,2,1,0:T(8,128)(2,1)}), bf16[4,2,64,768]{3,2,1,0:T(8,128)(2,1)S(1)}, u32[]{:S(2)}, u32[]{:S(2)}) async-start(bf16[4,2,64,768]{3,2,1,0:T(8,128)(2,1)} %copy.93), calls=%async_computation.5 | async-start | bytes 1572864 | tf_op jit(solution)/shard_map/all_to_all | solution.py:254
  814.0 15.3 %all-to-all-start.1 = ((bf16[4,2,64,768]{3,2,1,0:T(8,128)(2,1)}), bf16[4,2,64,768]{3,2,1,0:T(8,128)(2,1)S(1)}, u32[]{:S(2)}, u32[]{:S(2)}) async-start(bf16[4,2,64,768]{3,2,1,0:T(8,128)(2,1)} %copy.86), calls=%async_computation.1 | async-start | bytes 1572864 | tf_op jit(solution)/shard_map/all_to_all | solution.py:216
  817.6 108.0 %reduce-scatter.11.cloned.1.call-start = ((), (), s32[]{:S(2)}) async-start(), calls=%async_computation.25 | async-start | bytes 1966080 | tf_op jit(solution)/shard_map/reduce_scatter | solution.py:294
  844.4 81.2 %reduce-scatter.9.cloned.1.call-start = ((), (), s32[]{:S(2)}) async-start(), calls=%async_computation.24 | async-start | bytes 1966080 | tf_op jit(solution)/shard_map/reduce_scatter | solution.py:291
  871.3 60.7 %reduce-scatter.15.cloned.1.call-start = ((), (), s32[]{:S(2)}) async-start(), calls=%async_computation.27 | async-start | bytes 1966080 | tf_op jit(solution)/shard_map/reduce_scatter | solution.py:294
  880.1 83.5 %reduce-scatter.13.cloned.1.call-start = ((), (), s32[]{:S(2)}) async-start(), calls=%async_computation.26 | async-start | bytes 1966080 | tf_op jit(solution)/shard_map/reduce_scatter | solution.py:291
  907.2 266.8 %reduce-scatter.19.cloned.1.call-start = ((), (), s32[]{:S(2)}) async-start(), calls=%async_computation.29 | async-start | bytes 2433024 | tf_op jit(solution)/shard_map/reduce_scatter | solution.py:311
  910.7 284.4 %reduce-scatter.17.cloned.1.call-start = ((), (), s32[]{:S(2)}) async-start(), calls=%async_computation.28 | async-start | bytes 7299072 | tf_op jit(solution)/shard_map/reduce_scatter | solution.py:310
  971.1 390.3 %reduce-scatter.21.cloned.1.call-start = ((), (), s32[]{:S(2)}) async-start(), calls=%async_computation.30 | async-start | bytes 10616832 | tf_op jit(solution)/shard_map/reduce_scatter | solution.py:314
  1168.9 198.9 %copy-start.83 = (f32[32,12]{0,1:T(8,128)}, f32[32,12]{0,1:T(8,128)S(1)}, u32[]{:S(2)}) copy-start(f32[32,12]{0,1:T(8,128)S(1)} %get-tuple-element.204) | copy-start | bytes 4612
  1168.9 198.9 %copy-start.86 = (f32[2,768]{1,0:T(2,128)}, f32[2,768]{1,0:T(2,128)S(1)}, u32[]{:S(2)}) copy-start(f32[2,768]{1,0:T(2,128)S(1)} %get-tuple-element.203) | copy-start | bytes 18436
  1171.4 189.9 %copy-start.17 = (f32[2,96,3072]{2,1,0:T(8,128)S(1)}, f32[2,96,3072]{2,1,0:T(8,128)}, u32[]{:S(2)}) copy-start(f32[2,96,3072]{2,1,0:T(8,128)} %param.38) | copy-start | bytes 7077892
  (94 other events, 2085.7 us)
Sparse Core Ops, SparseCore 0:
  11.5 62.8 all-gather.10
  78.8 18.4 all-gather.12
  99.4 19.6 all-gather.14
  122.4 54.1 all-gather.16
  178.6 18.5 all-gather.22
  199.2 19.6 all-gather.24
  221.6 138.0 all-gather.18
  431.1 161.5 reduce-scatter.22
  599.4 137.1 all-gather.20
  844.5 25.4 reduce-scatter.10
  872.7 28.1 reduce-scatter.8
  903.9 28.1 reduce-scatter.14
  935.4 28.1 reduce-scatter.12
  969.3 99.0 reduce-scatter.18
  1075.4 119.6 reduce-scatter.16
  1198.6 162.7 reduce-scatter.20
where the time goes:
time: 1390 us; the launch traced here: 1370 us
  waiting for transfers between devices  727 us (52%)
  matrix products  337 us (24%)
  local copies, waits for them, and re-layouts  146 us (11%)
  other arithmetic  65.7 us (5%)
  blocking collectives  51.3 us (4%)
  starting transfers between devices  31.3 us (2%)
  between operations  15.9 us (1%)
    reduce_scatter x1, waiting for transfers between devices, local(): lax.psum_scatter(acc_in.astype(jnp.bfloat16), 'dp', scatter_dimension=1,...  164 us
    reduce_scatter x1, waiting for transfers between devices, local(): lax.psum_scatter(acc_out.astype(jnp.bfloat16), 'dp', scatter_dimension=1,...  161 us
    all_gather x1, waiting for transfers between devices, local(): lax.all_gather(out_low, 'dp', axis=1, tiled=True)  137 us
    all_gather x1, waiting for transfers between devices, local(): lax.all_gather(in_low, 'dp', axis=1, tiled=True)  118 us
    reshape x4, local copies, waits for them, and re-layouts, table_grad(): grad_logits.reshape(head_count, query_rows, block_count, block_width)  70.1 us
    all_gather x1, waiting for transfers between devices, local(): lax.all_gather(qkv_low, ('dp', 'expert'), axis=0, tiled=True)  62.7 us
    dot_general x4, matrix products, table_one_block(): jnp.einsum('uei,sei->su', current_piece, bucket_onehot_matrix(query_posit...  44.8 us
    psum x1, blocking collectives, local(): grad_gains, grad_bias = lax.psum((acc_gains, acc_table), ('dp', 'expert'))  41.2 us
  transfers between devices with their start and end apart: 24, of which 13 were waited for; matrix products, arithmetic and copies ran while one was open for 34% of the time, Pallas kernels for 0%

commit v1 on v0

v1 whole, which is shorter than its diff:
```python
import functools

import jax
import jax.numpy as jnp
from jax import lax
from jax.experimental import pallas as pl
from jax.experimental.pallas import tpu as pltpu
from jax.sharding import PartitionSpec as P

BUCKETS = 32
STEP = 10


EPS_NORM = 1e-06
MASKED = -1000000000.0
LIMITS = (12, 16, 23, 32, 46, 64, 91)
UPPER_PRECISION = lax.Precision.HIGHEST
LANES = 128
STRIP = 8
VMEM_BYTES = 48 * 1024 * 1024


def rms_norm(inputs, gain_vec):
    inv_rms = lax.rsqrt(jnp.mean(inputs * inputs, axis=-1, keepdims=True) + EPS_NORM)
    return inputs * inv_rms * gain_vec


def strip_onehot(first_query, tok_rows, seq_len):
    width = seq_len + tok_rows
    column = jnp.arange(width, dtype=jnp.int32)[None, :]
    row = jnp.arange(STRIP, dtype=jnp.int32)[:, None]
    offset = jnp.where(column >= seq_len, column - width, column) - row - first_query
    distance = jnp.abs(offset)
    far_bucket = 8 + sum(((distance >= bound_at).astype(jnp.int32) for bound_at in LIMITS))
    buckets = jnp.where(distance < 8, distance, far_bucket) + jnp.where(offset > 0, 16, 0)
    return (buckets[None] == jnp.arange(BUCKETS, dtype=jnp.int32)[:, None, None]).astype(
        jnp.float32
    )


def spread_bias(strip, rows, seq_len):
    grown = strip
    have = STRIP
    while have < rows:
        grown = jnp.concatenate([grown, pltpu.roll(grown, have, axis=1)], axis=0)
        have *= 2
    return grown[:, :seq_len]


def gather_bias(block, rows, width):
    left = jnp.concatenate(
        [block, jnp.zeros((rows, width - block.shape[1]), jnp.float32)], axis=1
    )
    have = rows
    while have > STRIP:
        have //= 2
        left = left[:have] + pltpu.roll(left[have:], width - have, axis=1)
    return left


def head_mask(which, head_dim):
    lane = lax.broadcasted_iota(jnp.int32, (1, LANES), 1)
    return ((lane >= which * head_dim) & (lane < (which + 1) * head_dim)).astype(jnp.float32)


def only_head(block, mask):
    return (block.astype(jnp.float32) * mask).astype(jnp.bfloat16)


def product(left, right, left_dim, right_dim):
    return lax.dot_general(
        left, right, (((left_dim,), (right_dim,)), ((), ())), preferred_element_type=jnp.float32
    )


def attend_kernel(head_dim, q_ref, k_ref, v_ref, sq_ref, sk_ref, strip_ref, o_ref, lse_ref):
    rows, seq_len = (q_ref.shape[1], k_ref.shape[1])
    allowed = sq_ref[0] == sk_ref[0]
    out = jnp.zeros((rows, LANES), jnp.float32)
    lse = jnp.zeros((rows, LANES), jnp.float32)
    for which in range(LANES // head_dim):
        mask = head_mask(which, head_dim)
        raw = product(only_head(q_ref[0], mask), k_ref[0], 1, 1)
        bias = spread_bias(strip_ref[which], rows, seq_len)
        logits = jnp.where(allowed, head_dim ** (-0.5) * raw + bias, MASKED)
        top = jnp.max(logits, axis=1, keepdims=True)
        weights = jnp.exp(logits - top)
        total = jnp.sum(weights, axis=1, keepdims=True)
        mixed = product(weights.astype(jnp.bfloat16), v_ref[0], 1, 0)
        out = out + mixed * (1.0 / total) * mask
        lse = lse + (top + jnp.log(total)) * mask
    o_ref[0] = out.astype(jnp.bfloat16)
    lse_ref[0] = lse


def attend_back_kernel(
    head_dim,
    q_ref,
    k_ref,
    v_ref,
    do_ref,
    lse_ref,
    sq_ref,
    sk_ref,
    strip_ref,
    dq_ref,
    dkv_ref,
    diag_ref,
):
    rows, seq_len = (q_ref.shape[1], k_ref.shape[1])
    width = strip_ref.shape[2]
    allowed = sq_ref[0] == sk_ref[0]
    grad_q = jnp.zeros((rows, LANES), jnp.float32)
    grad_k = jnp.zeros((seq_len, LANES), jnp.float32)
    grad_v = jnp.zeros((seq_len, LANES), jnp.float32)
    for which in range(LANES // head_dim):
        mask = head_mask(which, head_dim)
        raw = product(only_head(q_ref[0], mask), k_ref[0], 1, 1)
        bias = spread_bias(strip_ref[which], rows, seq_len)
        logits = jnp.where(allowed, head_dim ** (-0.5) * raw + bias, MASKED)
        lse = lse_ref[0, :, which * head_dim : which * head_dim + 1]
        probs = jnp.exp(logits - lse)
        grad_probs = product(only_head(do_ref[0], mask), v_ref[0], 1, 1)
        center = jnp.sum(probs * grad_probs, axis=1, keepdims=True)
        grad_logits = probs * (grad_probs - center)
        diag_ref[0, which] = gather_bias(grad_logits, rows, width)
        grad_raw = (head_dim ** (-0.5) * grad_logits).astype(jnp.bfloat16)
        grad_q = grad_q + product(grad_raw, k_ref[0], 1, 0) * mask
        grad_k = grad_k + product(grad_raw, q_ref[0], 0, 0) * mask
        grad_v = grad_v + product(probs.astype(jnp.bfloat16), do_ref[0], 0, 0) * mask
    dq_ref[0] = grad_q.astype(jnp.bfloat16)
    dkv_ref[0, 0] = grad_k.astype(jnp.bfloat16)
    dkv_ref[1, 0] = grad_v.astype(jnp.bfloat16)


def attention_specs(rows, seq_len, pairs, per_block, width):
    return dict(
        q=pl.BlockSpec((1, rows, LANES), lambda m, p: (m, 0, p)),
        k=pl.BlockSpec((1, seq_len, LANES), lambda m, p: (m, 0, p)),
        v=pl.BlockSpec((1, seq_len, LANES), lambda m, p: (m, 0, pairs + p)),
        sq=pl.BlockSpec((1, rows, 1), lambda m, p: (m, 0, 0)),
        sk=pl.BlockSpec((1, 1, seq_len), lambda m, p: (m, 0, 0)),
        strip=pl.BlockSpec((per_block, STRIP, width), lambda m, p: (p, 0, 0)),
    )


def attention(qkv_all, kv_all, seg_q, seg_k, strips, head_dim):
    micros, rows, _ = qkv_all.shape
    seq_len = kv_all.shape[1]
    heads, _, width = strips.shape
    model_width = heads * head_dim
    per_block = LANES // head_dim
    pairs = heads // per_block
    sp = attention_specs(rows, seq_len, pairs, per_block, width)
    return pl.pallas_call(
        functools.partial(attend_kernel, head_dim),
        grid=(micros, pairs),
        in_specs=[sp["q"], sp["k"], sp["v"], sp["sq"], sp["sk"], sp["strip"]],
        out_specs=[sp["q"], sp["q"]],
        out_shape=[
            jax.ShapeDtypeStruct((micros, rows, model_width), jnp.bfloat16),
            jax.ShapeDtypeStruct((micros, rows, model_width), jnp.float32),
        ],
        compiler_params=pltpu.CompilerParams(vmem_limit_bytes=VMEM_BYTES),
        cost_estimate=pl.CostEstimate(
            flops=16 * micros * heads * rows * seq_len * LANES,
            bytes_accessed=4 * micros * seq_len * model_width * 2,
            transcendentals=micros * heads * rows * seq_len,
        ),
    )(qkv_all, kv_all, kv_all, seg_q, seg_k, strips)


def attention_back(qkv_all, kv_all, grad_mixed, lse, seg_q, seg_k, strips, head_dim):
    micros, rows, _ = qkv_all.shape
    seq_len = kv_all.shape[1]
    heads, _, width = strips.shape
    model_width = heads * head_dim
    per_block = LANES // head_dim
    pairs = heads // per_block
    sp = attention_specs(rows, seq_len, pairs, per_block, width)
    return pl.pallas_call(
        functools.partial(attend_back_kernel, head_dim),
        grid=(micros, pairs),
        in_specs=[
            sp["q"], sp["k"], sp["v"], sp["q"], sp["q"], sp["sq"], sp["sk"], sp["strip"],
        ],
        out_specs=[
            sp["q"],
            pl.BlockSpec((2, 1, seq_len, LANES), lambda m, p: (0, m, 0, p)),
            pl.BlockSpec((1, per_block, STRIP, width), lambda m, p: (m, p, 0, 0)),
        ],
        out_shape=[
            jax.ShapeDtypeStruct((micros, rows, model_width), jnp.bfloat16),
            jax.ShapeDtypeStruct((2, micros, seq_len, model_width), jnp.bfloat16),
            jax.ShapeDtypeStruct((micros, heads, STRIP, width), jnp.float32),
        ],
        compiler_params=pltpu.CompilerParams(vmem_limit_bytes=VMEM_BYTES),
        cost_estimate=pl.CostEstimate(
            flops=40 * micros * heads * rows * seq_len * LANES,
            bytes_accessed=8 * micros * seq_len * model_width * 2,
            transcendentals=micros * heads * rows * seq_len,
        ),
    )(qkv_all, kv_all, kv_all, grad_mixed, lse, seg_q, seg_k, strips)


def slot_rank(chosen, expert_count):
    hot_rows = (chosen[:, :, None] == jnp.arange(expert_count, dtype=jnp.int32)).astype(jnp.int32)
    return jnp.sum((jnp.cumsum(hot_rows, axis=1) - 1) * hot_rows, axis=2)


def adam_step(weight, gradient, first_mom, second, step_rate):
    first_new = 0.9 * first_mom + 0.1 * gradient
    second_new = 0.999 * second + 0.001 * gradient * gradient
    first_hat = first_new / (1.0 - 0.9**STEP)
    second_hat = second_new / (1.0 - 0.999**STEP)
    updated = weight - step_rate * (first_hat / (jnp.sqrt(second_hat) + 1e-08) + 0.01 * weight)
    return (updated, second_new)


def local(
    tokens_in,
    out_grad,
    segments,
    expert_ids,
    gate_values,
    norm_gains,
    rel_bias,
    qkv_weight,
    proj_weight,
    expert_in,
    expert_out,
    first_gains,
    second_gains,
    first_bias,
    second_bias,
    first_qkv,
    second_qkv,
    first_proj,
    second_proj,
    first_in,
    second_in,
    first_out,
    second_out,
):
    groups = lax.axis_size("expert")
    slices = lax.axis_size("dp")
    micros, tok_rows, model_width = tokens_in.shape
    seq_len = tok_rows * groups
    head_count = rel_bias.shape[1]
    head_dim = model_width // head_count
    local_experts = expert_in.shape[0]
    expert_count = local_experts * groups
    capacity = 2 * tok_rows // expert_count
    hidden_units = expert_in.shape[2]
    own_rows = qkv_weight.shape[0]
    dense_width = 4 * model_width
    f32, bf16 = (jnp.float32, jnp.bfloat16)

    dense_low = jnp.concatenate([qkv_weight.astype(bf16), proj_weight.astype(bf16)], axis=1)
    dense_part = lax.all_gather(dense_low, "dp", axis=0, tiled=False)
    in_low, dense_part = lax.optimization_barrier((expert_in.astype(bf16), dense_part))
    dense_all = lax.all_gather(dense_part, "expert", axis=1, tiled=False).reshape(
        model_width, dense_width
    )
    dense_qkv = dense_all[:, : 3 * model_width]
    dense_proj = dense_all[:, 3 * model_width :]
    exp_in = lax.all_gather(in_low, "dp", axis=1, tiled=True)
    out_low, exp_in = lax.optimization_barrier((expert_out.astype(bf16), exp_in))
    exp_out = lax.all_gather(out_low, "dp", axis=1, tiled=True)

    onehot = strip_onehot(lax.axis_index("expert") * tok_rows, tok_rows, seq_len)
    strips = jnp.einsum("vg,vrc->grc", rel_bias, onehot, precision=UPPER_PRECISION)
    residual = tokens_in.astype(f32)
    normed, norm_back_one = jax.vjp(rms_norm, residual, norm_gains[0])
    act_one = normed.astype(bf16)
    qkv_all = jnp.einsum("mtd,df->mtf", act_one, dense_qkv, preferred_element_type=f32).astype(
        bf16
    )
    seg_cols = jnp.broadcast_to(segments.astype(bf16)[:, :, None], (micros, tok_rows, LANES))
    kv_all = lax.all_gather(
        jnp.concatenate([qkv_all[:, :, model_width:], seg_cols], axis=2),
        "expert",
        axis=1,
        tiled=True,
    )
    seg_q = segments.astype(f32)[:, :, None]
    seg_k = kv_all[:, :, 2 * model_width].astype(f32)[:, None, :]
    mixed_out, lse = attention(qkv_all, kv_all, seg_q, seg_k, strips, head_dim)
    hidden = residual + jnp.einsum(
        "mtd,df->mtf", mixed_out, dense_proj, preferred_element_type=f32
    )
    normed_two, norm_back_two = jax.vjp(rms_norm, hidden, norm_gains[1])

    chosen = expert_ids[:, :, 0]
    slot_rows = chosen * capacity + slot_rank(chosen, expert_count)
    place = (
        jnp.arange(expert_count * capacity, dtype=jnp.int32)[None, :, None]
        == slot_rows[:, None, :]
    ).astype(bf16)

    def to_experts(rows_low):
        buf = jnp.einsum("mst,mtd->msd", place, rows_low, preferred_element_type=f32).astype(bf16)
        buf = buf.reshape(micros, groups, local_experts, capacity, model_width)
        got = lax.all_to_all(buf, "expert", split_axis=1, concat_axis=1, tiled=True)
        return jnp.transpose(got, (2, 0, 1, 3, 4)).reshape(
            local_experts, micros * groups * capacity, model_width
        )

    def from_experts(rows_low):
        buf = jnp.transpose(
            rows_low.reshape(local_experts, micros, groups, capacity, model_width), (1, 2, 0, 3, 4)
        )
        got = lax.all_to_all(buf, "expert", split_axis=1, concat_axis=1, tiled=True)
        got = got.reshape(micros, expert_count * capacity, model_width)
        return jnp.einsum("mst,msd->mtd", place, got, preferred_element_type=f32)

    gate_col = gate_values[:, :, None]
    grad_top = out_grad.astype(f32)
    grad_res = to_experts((gate_col * grad_top).astype(bf16))
    arrived = to_experts(normed_two.astype(bf16))
    pre_act = jnp.einsum("ecd,edf->ecf", arrived, exp_in, preferred_element_type=f32)
    cdf = 0.5 * lax.erfc(-pre_act * (0.5**0.5))
    slope = cdf + pre_act * (jnp.exp(-0.5 * pre_act * pre_act) * 0.3989422804014327)
    post_act, slope = lax.optimization_barrier(
        ((pre_act * cdf).astype(bf16), slope.astype(bf16))
    )
    part_out = jnp.einsum(
        "ecf,ecd->efd", post_act, grad_res, preferred_element_type=f32
    ).astype(bf16)
    part_out, exp_out = lax.optimization_barrier((part_out, exp_out))
    grad_out = lax.psum_scatter(part_out, "dp", scatter_dimension=1, tiled=True).astype(f32)
    grad_post = jnp.einsum("ecd,efd->ecf", grad_res, exp_out, preferred_element_type=f32)
    grad_pre = (grad_post * slope.astype(f32)).astype(bf16)
    part_in = jnp.einsum("ecd,ecf->edf", arrived, grad_pre, preferred_element_type=f32).astype(
        bf16
    )
    grad_in = lax.psum_scatter(part_in, "dp", scatter_dimension=1, tiled=True).astype(f32)
    grad_back = from_experts(
        jnp.einsum("ecf,edf->ecd", grad_pre, exp_in, preferred_element_type=f32).astype(bf16)
    )
    result = from_experts(
        jnp.einsum("ecf,efd->ecd", post_act, exp_out, preferred_element_type=f32).astype(bf16)
    )
    block_out = hidden + gate_col * result

    grad_hidden_n, grad_gain_two = norm_back_two(grad_back)
    grad_hidden = grad_top + grad_hidden_n
    grad_attn = grad_hidden.astype(bf16)
    part_proj = jnp.einsum("mtd,mtf->df", mixed_out, grad_attn, preferred_element_type=f32)
    grad_mixed = jnp.einsum(
        "mtf,df->mtd", grad_attn, dense_proj, preferred_element_type=f32
    ).astype(bf16)
    grad_query, grad_kv, diag = attention_back(
        qkv_all, kv_all, grad_mixed, lse, seg_q, seg_k, strips, head_dim
    )
    part_table = jnp.einsum(
        "grc,vrc->vg", jnp.sum(diag, axis=0), onehot, precision=UPPER_PRECISION
    )
    kv_terms = lax.all_to_all(
        grad_kv.reshape(2, micros, groups, tok_rows, model_width),
        "expert",
        split_axis=2,
        concat_axis=2,
        tiled=True,
    )
    kv_sum = jnp.sum(kv_terms.astype(f32), axis=2).astype(bf16)
    grad_qkv_rows = jnp.concatenate([grad_query, kv_sum[0], kv_sum[1]], axis=2)
    part_qkv = jnp.einsum("mtd,mtf->df", act_one, grad_qkv_rows, preferred_element_type=f32)
    grad_normed = jnp.einsum(
        "mtf,df->mtd", grad_qkv_rows, dense_qkv, preferred_element_type=f32
    )
    grad_resid_n, grad_gain_one = norm_back_one(grad_normed)
    input_grad = grad_hidden + grad_resid_n

    part_dense = jnp.concatenate([part_qkv, part_proj], axis=1).astype(bf16)
    part_dense = lax.all_to_all(
        part_dense.reshape(slices, groups, own_rows, dense_width),
        "expert",
        split_axis=1,
        concat_axis=1,
        tiled=True,
    )
    part_dense = jnp.sum(part_dense.astype(f32), axis=1).astype(bf16)
    part_dense = lax.all_to_all(part_dense, "dp", split_axis=0, concat_axis=0, tiled=True)
    grad_dense = jnp.sum(part_dense.astype(f32), axis=0)
    grad_qkv = grad_dense[:, : 3 * model_width]
    grad_proj = grad_dense[:, 3 * model_width :]
    grad_gains, grad_bias = lax.psum(
        (jnp.stack([grad_gain_one, grad_gain_two]), part_table), ("dp", "expert")
    )
    fan_proj = max(1, 4 * model_width // seq_len)
    new_gains, moment_gains = adam_step(norm_gains, grad_gains, first_gains, second_gains, 0.25)
    updated_relative_bias, moment_bias = adam_step(
        rel_bias, grad_bias, first_bias, second_bias, 0.5
    )
    new_qkv, moment_qkv = adam_step(
        qkv_weight, grad_qkv, first_qkv, second_qkv, model_width ** (-0.5)
    )
    new_proj, moment_proj = adam_step(
        proj_weight, grad_proj, first_proj, second_proj, fan_proj ** (-0.5)
    )
    new_in, moment_in = adam_step(expert_in, grad_in, first_in, second_in, model_width ** (-0.5))
    new_out, moment_out = adam_step(
        expert_out, grad_out, first_out, second_out, (hidden_units // 2) ** (-0.5)
    )
    return (
        block_out,
        input_grad,
        grad_gains,
        grad_bias,
        grad_qkv,
        grad_proj,
        grad_in,
        grad_out,
        new_gains,
        updated_relative_bias,
        new_qkv,
        new_proj,
        new_in,
        new_out,
        moment_gains,
        moment_bias,
        moment_qkv,
        moment_proj,
        moment_in,
        moment_out,
    )


def solution(mesh):
    placed = (
        P(None, ("dp", "expert"), None),
        P(None, ("dp", "expert"), None),
        P(None, ("dp", "expert")),
        P(None, ("dp", "expert"), None),
        P(None, ("dp", "expert")),
        P(),
        P(),
        P(("dp", "expert"), None),
        P(("dp", "expert"), None),
        P("expert", "dp", None),
        P("expert", "dp", None),
        P(),
        P(),
        P(),
        P(),
        P(("dp", "expert"), None),
        P(("dp", "expert"), None),
        P(("dp", "expert"), None),
        P(("dp", "expert"), None),
        P("expert", "dp", None),
        P("expert", "dp", None),
        P("expert", "dp", None),
        P("expert", "dp", None),
    )
    return jax.shard_map(
        local,
        mesh=mesh,
        in_specs=placed,
        out_specs=(
            P(None, ("dp", "expert"), None),
            P(None, ("dp", "expert"), None),
            P(),
            P(),
            P(("dp", "expert"), None),
            P(("dp", "expert"), None),
            P("expert", "dp", None),
            P("expert", "dp", None),
            P(),
            P(),
            P(("dp", "expert"), None),
            P(("dp", "expert"), None),
            P("expert", "dp", None),
            P("expert", "dp", None),
            P(),
            P(),
            P(("dp", "expert"), None),
            P(("dp", "expert"), None),
            P("expert", "dp", None),
            P("expert", "dp", None),
        ),
        check_vma=False,
    )
```

time: 1390 us -> 823 us (0.59)
  waiting for transfers between devices: 727 us -> 467 us
  matrix products: 337 us -> 113 us
  local copies, waits for them, and re-layouts: 146 us -> 43.6 us
  Pallas kernels: 0 us -> 52.3 us
  other arithmetic: 65.7 us -> 47.7 us
    reduce_scatter x8 -> x2, waiting for transfers between devices: 378 us -> 23.2 us  [the longest x1 23.2 us: local(): lax.psum_scatter(part_out, 'dp', scatter_dimension=1, tiled=True)]
    dot_general x40 -> x18, matrix products: 297 us -> 113 us  [the longest x1 35.9 us: local(): jnp.einsum('ecd,edf->ecf', arrived, exp_in, preferred_element_type=f32)]
    all_to_all x8 -> x7, waiting for transfers between devices: 8.49 us -> 152 us  [the longest x1 56.5 us: local(): lax.all_to_all(grad_kv.reshape(2, micros, groups, tok_rows, model_width),...]
    reshape x9 -> x5, local copies, waits for them, and re-layouts: 88.4 us -> 11 us  [the longest x1 5.9 us: local(): grad_kv.reshape(2, micros, groups, tok_rows, model_width)]
    pallas_call x0 -> x2, Pallas kernels: none -> 52.3 us  [the longest x1 32.3 us: attention_back(): pl.pallas_call(functools.partial(attend_back_kernel, head_dim), grid=(mic...]
    all_gather x8 -> x5, waiting for transfers between devices: 339 us -> 290 us  [the longest x1 132 us: local(): exp_in = lax.all_gather(in_low, 'dp', axis=1, tiled=True)]
    sub x2 -> x0, matrix products: 39.1 us -> none  [local(): grad_probs - jnp.sum(attn_probs * grad_probs, axis=-1, keepdims=True)]
    transpose x1 -> x2, local copies, waits for them, and re-layouts: 22.5 us -> 2.79 us  [to_experts(): jnp.transpose(got, (2, 0, 1, 3, 4))]
  transfers between devices with their start and end apart: 24 -> 14, of which waited for: 13 -> 11; matrix products, arithmetic and copies ran while one was open for 34% -> 21% of each run, Pallas kernels for 0% -> 6%
where the time goes in v1:
time: 823 us; the launch traced here: 815 us
  waiting for transfers between devices  467 us (57%)
  matrix products  113 us (14%)
  Pallas kernels  52.3 us (6%)
  other arithmetic  47.7 us (6%)
  local copies, waits for them, and re-layouts  43.6 us (5%)
  blocking collectives  43.6 us (5%)
  starting transfers between devices  31.9 us (4%)
  between operations  15.6 us (2%)
    all_gather x1, waiting for transfers between devices, local(): exp_in = lax.all_gather(in_low, 'dp', axis=1, tiled=True)  132 us
    all_to_all x1, waiting for transfers between devices, local(): lax.all_to_all(grad_kv.reshape(2, micros, groups, tok_rows, model_width),...  56.5 us
    all_gather x1, waiting for transfers between devices, local(): lax.all_gather(jnp.concatenate([qkv_all[:, :, model_width:], seg_cols], a...  54.9 us
    all_to_all x1, waiting for transfers between devices, local(): lax.all_to_all(part_dense.reshape(slices, groups, own_rows, dense_width),...  51.1 us
    psum x1, blocking collectives, local(): lax.psum((jnp.stack([grad_gain_one, grad_gain_two]), part_table), ('dp',...  43.6 us
    all_gather x1, waiting for transfers between devices, local(): dense_part = lax.all_gather(dense_low, 'dp', axis=0, tiled=False)  41.8 us
    all_gather x1, waiting for transfers between devices, local(): lax.all_gather(dense_part, 'expert', axis=1, tiled=False)  36.7 us
    dot_general x1, matrix products, local(): jnp.einsum('ecd,edf->ecf', arrived, exp_in, preferred_element_type=f32)  35.9 us
  transfers between devices with their start and end apart: 14, of which 11 were waited for; matrix products, arithmetic and copies ran while one was open for 21% of the time, Pallas kernels for 6%

profile of v1, /device:TPU:0, one launch (start us, length us, event | category | flops | bytes accessed | tf_op | source)
XLA Modules:
  0.0 814.5 jit_solution(1172057273558448977)
XLA Ops:
  12.8 41.8 %all-gather.14.cloned.1.call-done = bf16[192,3072]{1,0:T(8,128)(2,1)} async-done(((bf16[24,3072]{1,0:T(8,128)(2,1)}), bf16[192,3072]{1,0:T(8,128)(2,1)}) %all-gather.14.cloned.1.call-update) | async-done | bytes 1179664 | tf_op jit(solution)/shard_map/all_gather | solution.py:260
  55.7 36.7 %all-gather.16.cloned.1.call-done = bf16[8,96,3072]{2,1,0:T(8,128)(2,1)} async-done(((bf16[8,24,3072]{2,1,0:T(8,128)(2,1)}), bf16[8,96,3072]{2,1,0:T(8,128)(2,1)}) %all-gather.16.cloned.1.call-update) | async-done | bytes 4718608 | tf_op jit(solution)/shard_map/all_gather | solution.py:262
  101.4 131.9 %all-gather.10.cloned.1.call-done = bf16[2,768,3072]{2,1,0:T(8,128)(2,1)} async-done(((bf16[2,96,3072]{2,1,0:T(8,128)(2,1)}), bf16[2,768,3072]{2,1,0:T(8,128)(2,1)}) %all-gather.10.cloned.1.call-update) | async-done | bytes 9437200 | tf_op jit(solution)/shard_map/all_gather | solution.py:267
  236.9 4.5 all-to-all-start.1
  245.7 54.9 %all-gather.8.cloned.1.call-done = bf16[2,1024,1664]{1,2,0:T(8,128)(2,1)} async-done(((bf16[2,256,1664]{1,2,0:T(8,128)(2,1)}), bf16[2,1024,1664]{1,2,0:T(8,128)(2,1)}) %all-gather.8.cloned.1.call-update) | async-done | bytes 6815760 | tf_op jit(solution)/shard_map/all_gather | solution.py:280
  300.6 9.8 %copy.112.k_ref.v_ref = bf16[2,1024,1664]{2,1,0:T(8,128)(2,1)} copy(bf16[2,1024,1664]{1,2,0:T(8,128)(2,1)} %all-gather.8.cloned.1.call-done) | data formatting | bytes 13631488 | tf_op jit(solution)/shard_map/all_gather | solution.py:280
  311.2 20.0 %shard_map.374 = (bf16[2,256,768]{2,1,0:T(8,128)(2,1)S(1)}, f32[2,256,768]{2,1,0:T(8,128)S(1)}) custom-call(bf16[2,256,2304]{2,1,0:T(8,128)(2,1)S(1)} %copy.111.q_ref, bf16[2,1024,1664]{2,1,0:T(8,128)(2,1)} %copy.112.k_ref.v_ref, bf16[2,1024,1664]{2,1,0:T(8,128)(2,1)} %copy.112.k_ref.v_ref, f32[2,256,1]{2,1,0:T(8,128)S(1)} %copy.114.sq_ref, ...), custom_call_target="tpu_custom_call" | custom-call | flops 12884901888 | bytes 12582912 | tf_op jit(solution)/shard_map/pallas_call | solution.py:155
  343.8 17.3 %all-to-all-done = bf16[2,4,2,64,768]{4,3,2,0,1:T(8,128)(2,1)S(1)} async-done(((bf16[2,4,2,64,768]{4,3,2,0,1:T(8,128)(2,1)}), bf16[2,4,2,64,768]{4,3,2,0,1:T(8,128)(2,1)S(1)}, u32[]{:S(2)}, u32[]{:S(2)}) %all-to-all-start) | async-done | bytes 1572896 | tf_op jit(solution)/shard_map/all_to_all | solution.py:304
  361.3 35.9 %fusion.6 = (bf16[2,512,3072]{2,1,0:T(8,128)(2,1)}, f32[2,512,3072]{2,1,0:T(8,128)S(1)}, f32[2,512,3072]{2,1,0:T(8,128)S(1)}) fusion(bf16[2,512,768]{2,1,0:T(8,128)(2,1)S(1)} %bitcast.97, bf16[2,768,3072]{2,1,0:T(8,128)(2,1)} %all-gather.10.cloned.1.call-done), kind=kOutput, calls=%fused_computation.8 | convolution fusion | flops 5048893440 | bytes 42467328 | tf_op jit(solution)/shard_map/ecd,edf->ecf/dot_general | solution.py:321
  401.5 12.3 %convolution_convert_fusion.1 = bf16[2,3072,768]{2,1,0:T(8,128)(2,1)} fusion(bf16[2,512,3072]{2,1,0:T(8,128)(2,1)} %multiply_convert_fusion.1, bf16[2,512,768]{2,1,0:T(8,128)(2,1)S(1)} %bitcast.95), kind=kOutput, calls=%fused_computation.27 | convolution fusion | flops 4836556800 | bytes 17301504 | tf_op jit(solution)/shard_map/ecf,ecd->efd/dot_general | solution.py:327
  413.8 24.7 %all-gather.12.cloned.1.call-done = bf16[2,3072,768]{2,1,0:T(8,128)(2,1)} async-done(((bf16[2,384,768]{2,1,0:T(8,128)(2,1)}), bf16[2,3072,768]{2,1,0:T(8,128)(2,1)}) %all-gather.12.cloned.1.call-update) | async-done | bytes 9437200 | tf_op jit(solution)/shard_map/all_gather | solution.py:269
  438.6 10.1 %multiply_convert_fusion = bf16[2,512,3072]{2,1,0:T(8,128)(2,1)S(1)} fusion(bf16[2,512,3072]{2,1,0:T(8,128)(2,1)} %get-tuple-element.40, bf16[2,512,768]{2,1,0:T(8,128)(2,1)S(1)} %bitcast.96, bf16[2,3072,768]{2,1,0:T(8,128)(2,1)} %all-gather.12.cloned.1.call-done), kind=kOutput, calls=%fused_computation.9 | convolution fusion | flops 4841275392 | bytes 23592960 | tf_op jit(solution)/shard_map/ecd,efd->ecf/dot_general | solution.py:332
  451.3 7.6 convolution_convert_fusion
  458.9 10.0 %convolution_convert_fusion.3 = bf16[2,512,768]{2,1,0:T(8,128)(2,1)S(1)} fusion(bf16[2,512,3072]{2,1,0:T(8,128)(2,1)} %copy-done.60, bf16[2,768,3072]{2,1,0:T(8,128)(2,1)} %all-gather.10.cloned.1.call-done), kind=kOutput, calls=%fused_computation.53 | convolution fusion | flops 4832624640 | bytes 17301504 | tf_op jit(solution)/shard_map/ecf,edf->ecd/dot_general | solution.py:339
  475.3 19.3 %all-to-all-done.3 = bf16[2,4,2,64,768]{4,3,0,2,1:T(8,128)(2,1)} async-done(((bf16[2,4,2,64,768]{4,3,0,2,1:T(8,128)(2,1)}), bf16[2,4,2,64,768]{4,3,0,2,1:T(8,128)(2,1)}, u32[]{:S(2)}, u32[]{:S(2)}) %all-to-all-start.3) | async-done | bytes 1572896 | tf_op jit(solution)/shard_map/all_to_all | solution.py:313
  500.6 32.3 %shard_map.375 = (bf16[2,256,768]{2,1,0:T(8,128)(2,1)S(1)}, bf16[2,2,1024,768]{3,2,1,0:T(8,128)(2,1)}, f32[2,12,8,1280]{3,2,1,0:T(8,128)S(1)}) custom-call(bf16[2,256,2304]{2,1,0:T(8,128)(2,1)} %copy-done, bf16[2,1024,1664]{2,1,0:T(8,128)(2,1)} %copy.112.k_ref.v_ref, bf16[2,1024,1664]{2,1,0:T(8,128)(2,1)} %copy.112.k_ref.v_ref, ...), custom_call_target="tpu_custom_call" | custom-call | flops 32212254720 | bytes 25165824 | tf_op jit(solution)/shard_map/pallas_call | solution.py:181
  532.8 5.9 copy.130
  538.7 5.3 all-to-all-start.4
  544.0 10.1 %convolution_convert_fusion.4 = bf16[2,512,768]{2,1,0:T(8,128)(2,1)S(1)} fusion(bf16[2,512,3072]{2,1,0:T(8,128)(2,1)} %multiply_convert_fusion.1, bf16[2,3072,768]{2,1,0:T(8,128)(2,1)} %all-gather.12.cloned.1.call-done), kind=kOutput, calls=%fused_computation.54 | convolution fusion | flops 4832624640 | bytes 17301504 | tf_op jit(solution)/shard_map/ecf,efd->ecd/dot_general | solution.py:342
  558.2 56.5 %all-to-all-done.4 = bf16[2,2,4,256,768]{4,3,1,0,2:T(8,128)(2,1)} async-done(((bf16[2,2,4,256,768]{4,3,1,0,2:T(8,128)(2,1)}), bf16[2,2,4,256,768]{4,3,1,0,2:T(8,128)(2,1)}, u32[]{:S(2)}, u32[]{:S(2)}) %all-to-all-start.4) | async-done | bytes 6291488 | tf_op jit(solution)/shard_map/all_to_all | solution.py:359
  614.8 4.5 all-to-all-start.2
  619.3 5.3 reduce_sum.125
  631.8 7.6 all-to-all-done.2
  639.4 5.0 all-to-all-start.5
  647.1 51.1 %all-to-all-done.5 = bf16[8,4,24,3072]{3,2,0,1:T(8,128)(2,1)} async-done(((bf16[8,4,24,3072]{3,2,0,1:T(8,128)(2,1)}), bf16[8,4,24,3072]{3,2,0,1:T(8,128)(2,1)}, u32[]{:S(2)}, u32[]{:S(2)}) %all-to-all-start.5) | async-done | bytes 4718624 | tf_op jit(solution)/shard_map/all_to_all | solution.py:376
  698.3 4.6 reduce_sum.130
  702.8 4.4 all-to-all-start.6
  712.0 6.1 fusion.19
  718.1 43.6 %all-reduce = (f32[2,768]{1,0:T(2,128)S(1)}, f32[32,12]{0,1:T(8,128)S(1)}) all-reduce(f32[2,768]{1,0:T(2,128)S(1)} %pad_maximum_fusion.6, f32[32,12]{0,1:T(8,128)S(1)} %fusion.26), channel_id=1, replica_groups=mesh['dp'=8,'expert'=4] {'dp','expert'}, use_global_device_ids=true, to_apply=%region_10.11 | all-reduce | flops 1920 | bytes 15360 | tf_op jit(solution)/shard_map/psum | solution.py:388
  770.7 6.5 multiply_subtract_fusion.1
  777.2 23.2 %reduce-scatter.5.cloned.1.call-done = bf16[2,384,768]{2,1,0:T(8,128)(2,1)} async-done(((bf16[2,3072,768]{2,1,0:T(8,128)(2,1)}), bf16[2,384,768]{2,1,0:T(8,128)(2,1)}) %reduce-scatter.5.cloned.1.call-update) | async-done | bytes 1179664 | tf_op jit(solution)/shard_map/reduce_scatter | solution.py:331
  800.4 6.9 multiply_subtract_fusion
  (204 shorter events, 83.3 us)
Async XLA Ops:
  7.2 47.4 %all-gather.14.cloned.1.call-start = ((), (), s32[]{:S(2)}) async-start(), calls=%async_computation.14 | async-start | bytes 1327104 | tf_op jit(solution)/shard_map/all_gather | solution.py:260
  9.8 45.6 %copy-start.40 = (f32[2,768]{1,0:T(2,128)S(1)}, f32[2,768]{1,0:T(2,128)}, u32[]{:S(2)}) copy-start(f32[2,768]{1,0:T(2,128)} %param.28) | copy-start | bytes 18436
  9.8 45.6 %copy-start.16 = (bf16[2,256,768]{2,1,0:T(8,128)(2,1)S(1)}, bf16[2,256,768]{2,1,0:T(8,128)(2,1)}, u32[]{:S(2)}) copy-start(bf16[2,256,768]{2,1,0:T(8,128)(2,1)} %param.23) | copy-start | bytes 2359300
  9.8 82.6 %all-gather.16.cloned.1.call-start = ((), (), s32[]{:S(2)}) async-start(), calls=%async_computation.15 | async-start | bytes 5898240 | tf_op jit(solution)/shard_map/all_gather | solution.py:262
  12.8 43.0 %copy-start.59 = (s32[2,256]{1,0:T(2,128)S(1)}, s32[2,256]{1,0:T(2,128)}, u32[]{:S(2)}) copy-start(s32[2,256]{1,0:T(2,128)} %param.25) | copy-start | bytes 6148
  54.6 178.7 %all-gather.10.cloned.1.call-start = ((), (), s32[]{:S(2)}) async-start(), calls=%async_computation.10 | async-start | bytes 10616832 | tf_op jit(solution)/shard_map/all_gather | solution.py:267
  55.3 245.3 %all-gather.8.cloned.1.call-start = ((), (), s32[]{:S(2)}) async-start(), calls=%async_computation.9 | async-start | bytes 8519680 | tf_op jit(solution)/shard_map/all_gather | solution.py:280
  55.4 41.1 %copy-start.45 = (f32[768]{0:T(1024)}, f32[768]{0:T(1024)S(1)}, u32[]{:S(2)}) copy-start(f32[768]{0:T(1024)S(1)} %get-tuple-element.51) | copy-start | bytes 9220
  55.4 278.9 %copy-start.32 = (f32[768]{0:T(1024)}, f32[768]{0:T(1024)S(1)}, u32[]{:S(2)}) copy-start(f32[768]{0:T(1024)S(1)} %get-tuple-element.50) | copy-start | bytes 9220
  99.3 134.0 %copy-start.44 = (s32[2,256,1]{1,2,0:T(1,128)S(1)}, s32[2,256,1]{1,2,0:T(1,128)}, u32[]{:S(2)}) copy-start(s32[2,256,1]{1,2,0:T(1,128)} %param.26) | copy-start | bytes 6148
  99.3 135.5 %copy-start.19 = (bf16[2,256,768]{2,1,0:T(8,128)(2,1)S(1)}, bf16[2,256,768]{2,1,0:T(8,128)(2,1)}, u32[]{:S(2)}) copy-start(bf16[2,256,768]{2,1,0:T(8,128)(2,1)} %param.24) | copy-start | bytes 2359300
  99.3 135.5 %copy-start.47 = (f32[2,256]{1,0:T(2,128)S(1)}, f32[2,256]{1,0:T(2,128)}, u32[]{:S(2)}) copy-start(f32[2,256]{1,0:T(2,128)} %param.27) | copy-start | bytes 6148
  99.3 339.2 %all-gather.12.cloned.1.call-start = ((), (), s32[]{:S(2)}) async-start(), calls=%async_computation.11 | async-start | bytes 10616832 | tf_op jit(solution)/shard_map/all_gather | solution.py:269
  234.9 99.5 %copy-start.34 = (s32[2,256]{1,0:T(2,128)}, s32[2,256]{1,0:T(2,128)S(1)}, u32[]{:S(2)}) copy-start(s32[2,256]{1,0:T(2,128)S(1)} %multiply_add_fusion.2) | copy-start | bytes 6148
  236.9 100.6 %all-to-all-start.1 = ((bf16[2,4,2,64,768]{4,3,2,0,1:T(8,128)(2,1)}), bf16[2,4,2,64,768]{4,3,2,0,1:T(8,128)(2,1)}, u32[]{:S(2)}, u32[]{:S(2)}) async-start(bf16[2,4,2,64,768]{4,3,2,0,1:T(8,128)(2,1)} %copy.119), calls=%async_computation.1 | async-start | bytes 3145728 | tf_op jit(solution)/shard_map/all_to_all | solution.py:304
  245.7 65.5 %copy-start = (bf16[2,256,2304]{2,1,0:T(8,128)(2,1)}, bf16[2,256,2304]{2,1,0:T(8,128)(2,1)S(1)}, u32[]{:S(2)}) copy-start(bf16[2,256,2304]{2,1,0:T(8,128)(2,1)S(1)} %copy.111.q_ref) | copy-start | bytes 7077892
  337.5 23.6 %all-to-all-start = ((bf16[2,4,2,64,768]{4,3,2,0,1:T(8,128)(2,1)}), bf16[2,4,2,64,768]{4,3,2,0,1:T(8,128)(2,1)S(1)}, u32[]{:S(2)}, u32[]{:S(2)}) async-start(bf16[2,4,2,64,768]{4,3,2,0,1:T(8,128)(2,1)} %copy.116), calls=%async_computation | async-start | bytes 3145728 | tf_op jit(solution)/shard_map/all_to_all | solution.py:304
  341.1 429.6 %reduce-scatter.3.cloned.1.call-start = ((), (), s32[]{:S(2)}) async-start(), calls=%async_computation.12 | async-start | bytes 10616832 | tf_op jit(solution)/shard_map/reduce_scatter | solution.py:337
  470.1 24.5 %all-to-all-start.3 = ((bf16[2,4,2,64,768]{4,3,0,2,1:T(8,128)(2,1)}), bf16[2,4,2,64,768]{4,3,0,2,1:T(8,128)(2,1)}, u32[]{:S(2)}, u32[]{:S(2)}) async-start(bf16[2,4,2,64,768]{4,3,0,2,1:T(8,128)(2,1)} %bitcast.80), calls=%async_computation.3 | async-start | bytes 3145728 | tf_op jit(solution)/shard_map/all_to_all | solution.py:313
  474.5 325.9 %reduce-scatter.5.cloned.1.call-start = ((), (), s32[]{:S(2)}) async-start(), calls=%async_computation.13 | async-start | bytes 10616832 | tf_op jit(solution)/shard_map/reduce_scatter | solution.py:331
  538.7 76.0 %all-to-all-start.4 = ((bf16[2,2,4,256,768]{4,3,1,0,2:T(8,128)(2,1)}), bf16[2,2,4,256,768]{4,3,1,0,2:T(8,128)(2,1)}, u32[]{:S(2)}, u32[]{:S(2)}) async-start(bf16[2,2,4,256,768]{4,3,1,0,2:T(8,128)(2,1)} %copy.130), calls=%async_computation.4 | async-start | bytes 12582912 | tf_op jit(solution)/shard_map/all_to_all | solution.py:359
  614.8 24.7 %all-to-all-start.2 = ((bf16[2,4,2,64,768]{4,3,0,2,1:T(8,128)(2,1)}), bf16[2,4,2,64,768]{4,3,0,2,1:T(8,128)(2,1)}, u32[]{:S(2)}, u32[]{:S(2)}) async-start(bf16[2,4,2,64,768]{4,3,0,2,1:T(8,128)(2,1)} %bitcast.87), calls=%async_computation.2 | async-start | bytes 3145728 | tf_op jit(solution)/shard_map/all_to_all | solution.py:313
  639.4 58.8 %all-to-all-start.5 = ((bf16[8,4,24,3072]{3,2,0,1:T(8,128)(2,1)}), bf16[8,4,24,3072]{3,2,0,1:T(8,128)(2,1)}, u32[]{:S(2)}, u32[]{:S(2)}) async-start(bf16[8,4,24,3072]{3,2,0,1:T(8,128)(2,1)} %copy.144), calls=%async_computation.5 | async-start | bytes 9437184 | tf_op jit(solution)/shard_map/all_to_all | solution.py:376
  702.8 63.6 %all-to-all-start.6 = ((bf16[8,24,3072]{2,1,0:T(8,128)(2,1)}), bf16[8,24,3072]{2,1,0:T(8,128)(2,1)}, u32[]{:S(2)}, u32[]{:S(2)}) async-start(bf16[8,24,3072]{2,1,0:T(8,128)(2,1)} %reduce_sum.130), calls=%async_computation.6 | async-start | bytes 2359296 | tf_op jit(solution)/shard_map/all_to_all | solution.py:384
  712.0 49.8 %copy-start.43 = (f32[2,256]{1,0:T(2,128)S(1)}, f32[2,256]{1,0:T(2,128)}, u32[]{:S(2)}) copy-start(f32[2,256]{1,0:T(2,128)} %copy-done.42) | copy-start | bytes 6148
  712.0 49.8 %copy-start.41 = (f32[2,768]{1,0:T(2,128)S(1)}, f32[2,768]{1,0:T(2,128)}, u32[]{:S(2)}) copy-start(f32[2,768]{1,0:T(2,128)} %param.28) | copy-start | bytes 18436
  712.0 49.8 %copy-start.56 = (f32[2,768]{1,0:T(2,128)S(1)}, f32[2,768]{1,0:T(2,128)}, u32[]{:S(2)}) copy-start(f32[2,768]{1,0:T(2,128)} %param.34) | copy-start | bytes 18436
  712.0 49.8 %copy-start.57 = (f32[2,768]{1,0:T(2,128)S(1)}, f32[2,768]{1,0:T(2,128)}, u32[]{:S(2)}) copy-start(f32[2,768]{1,0:T(2,128)} %param.35) | copy-start | bytes 18436
  712.0 50.5 %copy-start.39 = (f32[32,12]{0,1:T(8,128)S(1)}, f32[32,12]{0,1:T(8,128)}, u32[]{:S(2)}) copy-start(f32[32,12]{0,1:T(8,128)} %param.29) | copy-start | bytes 4612
  712.0 50.5 %copy-start.53 = (f32[32,12]{0,1:T(8,128)S(1)}, f32[32,12]{0,1:T(8,128)}, u32[]{:S(2)}) copy-start(f32[32,12]{0,1:T(8,128)} %param.36) | copy-start | bytes 4612
  712.0 50.4 %copy-start.54 = (f32[32,12]{0,1:T(8,128)S(1)}, f32[32,12]{0,1:T(8,128)}, u32[]{:S(2)}) copy-start(f32[32,12]{0,1:T(8,128)} %param.37) | copy-start | bytes 4612
  712.0 51.1 %copy-start.11 = (f32[2,256,768]{2,1,0:T(8,128)S(1)}, f32[2,256,768]{2,1,0:T(8,128)}, u32[]{:S(2)}) copy-start(f32[2,256,768]{2,1,0:T(8,128)} %copy-done.9) | copy-start | bytes 4718596
  (43 other events, 375.9 us)
Sparse Core Ops, SparseCore 0:
  10.8 43.7 all-gather.13
  56.1 36.2 all-gather.15
  95.2 138.0 all-gather.9
  235.2 65.2 all-gather.7
  303.2 135.3 all-gather.11
  459.0 161.4 reduce-scatter.2
  624.1 176.2 reduce-scatter.4
